TPU v7x, 32 devices: a whole 2x2x4 slice. The times are simulated.
32 devices in a mesh: space: 4 (over x, core), energy: 8 (over z, y).
Axes of the slice: x: 2, y: 2, z: 4, core: 2. Of those that a mesh axis runs over, the one named last changes fastest.
Arguments:
- green_lower: bfloat16 [4, 32, 2, 128, 128], P('space', 'energy'), may hold values from -0.5 to 0.5
- green_diag: bfloat16 [4, 32, 2, 128, 128], P('space', 'energy'), may hold values from -0.5 to 0.5
- green_upper: bfloat16 [4, 32, 2, 128, 128], P('space', 'energy'), may hold values from -0.5 to 0.5
- self_energy: bfloat16 [2, 4, 32, 2, 128, 128], P(None, 'space', 'energy'), may hold values from -1.75 to 1.75
- coulomb: bfloat16 [4, 128, 128], P('space'), may hold values from -0.5 to 0.5
Outputs:
- screened_polarization: bfloat16 [2, 4, 32, 2, 128, 128], P(None, 'space', 'energy')
All inputs are finite; a program needn't handle non-finite values.
Results may differ from a plain program's by a relative error of at most 0.017.
Values may be sent and summed in bfloat16 or wider, within the bound.
A program may use at most 64 MiB of HBM per device.

v0:
```python
import math

import jax
import jax.numpy as jnp
from jax import lax
from jax.sharding import PartitionSpec as P


def padded_2(shard, sides, width):
    for axis, dim in sides:
        peers, length = (lax.axis_size(axis), shard.shape[dim])
        up = [(i, (i + 1) % peers) for i in range(peers - 1)]
        down = [(j, i) for i, j in up]
        last = lax.slice_in_dim(shard, length - width, length, axis=dim)
        initial = lax.slice_in_dim(shard, 0, width, axis=dim)
        before = lax.ppermute(last, axis, up)
        after = lax.ppermute(initial, axis, down)
        shard = jnp.concatenate([before, shard, after], axis=dim)
    return shard


def congruence(green, sigma):
    green_real = green[:, :, 0]
    green_imag = green[:, :, 1]
    sigma_real = sigma[:, :, :, 0]
    sigma_imag = sigma[:, :, :, 1]
    green_wide = jnp.concatenate([green_real, green_imag], axis=-1)
    sigma_tall = jnp.concatenate(
        [
            jnp.concatenate([sigma_real, sigma_imag], axis=-1),
            jnp.concatenate([-sigma_imag, sigma_real], axis=-1),
        ],
        axis=-2,
    )
    mixed = jnp.einsum(
        "nepq,fneqr->fnepr", green_wide, sigma_tall, preferred_element_type=jnp.float32
    ).astype(jnp.bfloat16)
    adjoint_tall = jnp.concatenate(
        [green_wide, jnp.concatenate([-green_imag, green_real], axis=-1)], axis=-2
    )
    return jnp.einsum("fnepr,nesr->fneps", mixed, adjoint_tall, preferred_element_type=jnp.float32)


def split_table(table):
    high_part = table.astype(jnp.bfloat16)
    low_part = (table - high_part.astype(jnp.float32)).astype(jnp.bfloat16)
    return (high_part, low_part)


def spectrum(values, table_high, table_low, padded_len):

    def apply_table(part):
        return jnp.dot(table_high, part, preferred_element_type=jnp.float32) + jnp.dot(
            table_low, part, preferred_element_type=jnp.float32
        )

    real_terms = apply_table(values[:, 0])
    imag_terms = apply_table(values[:, 1])
    out_real = real_terms[:padded_len] + imag_terms[padded_len:]
    out_imag = imag_terms[:padded_len] - real_terms[padded_len:]
    return (out_real, out_imag)


def body(green_lower, green_diag, green_upper, self_energy, coulomb):
    block_count = green_diag.shape[0]
    energy_local = green_diag.shape[1]
    block_order = green_diag.shape[-1]
    energies = energy_local * lax.axis_size("energy")
    padded_len = 2 * energies
    padded = padded_2(self_energy, (("space", 1),), 1)
    lower_term = congruence(green_lower, padded[:, :block_count])
    diag_term = congruence(green_diag, padded[:, 1 : block_count + 1])
    upper_term = congruence(green_upper, padded[:, 2:])
    total = lower_term + diag_term + upper_term
    total = total.reshape(2, block_count, energy_local, block_order, 2, block_order)
    green_function = (
        jnp.transpose(total, (0, 2, 4, 1, 3, 5))
        .astype(jnp.bfloat16)
        .reshape(2, energy_local, 2, -1)
    )
    frequency = lax.iota(jnp.int32, padded_len)
    energy_index = lax.iota(jnp.int32, energies)
    step_angle = 2.0 * math.pi / padded_len
    forward_angle = (frequency[:, None] * energy_index[None, :] % padded_len).astype(
        jnp.float32
    ) * step_angle
    forward_table = jnp.concatenate([jnp.cos(forward_angle), jnp.sin(forward_angle)], axis=0)
    table_high, table_low = split_table(forward_table)
    lesser_values = lax.all_to_all(
        green_function[0], "energy", split_axis=2, concat_axis=0, tiled=True
    )
    greater_values = lax.all_to_all(
        green_function[1], "energy", split_axis=2, concat_axis=0, tiled=True
    )
    lesser_real, lesser_imag = spectrum(lesser_values, table_high, table_low, padded_len)
    greater_real, greater_imag = spectrum(greater_values, table_high, table_low, padded_len)
    product_real = lesser_real * greater_real + lesser_imag * greater_imag
    product_imag = lesser_imag * greater_real - lesser_real * greater_imag
    row_index = jnp.concatenate([energy_index, (padded_len - energy_index) % padded_len])
    back_angle = (row_index[:, None] * frequency[None, :] % padded_len).astype(
        jnp.float32
    ) * step_angle
    back_cos = jnp.cos(back_angle)
    back_sin = jnp.sin(back_angle)
    back_table = jnp.concatenate(
        [
            jnp.concatenate([back_cos, -back_sin], axis=1),
            jnp.concatenate([back_sin, back_cos], axis=1),
        ],
        axis=0,
    )
    stacked_product = jnp.concatenate([product_real, product_imag], axis=0)
    factor = 1.0 / (padded_len * math.sqrt(energies))
    combined = (
        jnp.dot(
            back_table,
            stacked_product,
            precision=lax.Precision.HIGH,
            preferred_element_type=jnp.float32,
        )
        * factor
    )
    corr_real = combined[:padded_len]
    corr_imag = combined[padded_len:]
    lesser_lags = jnp.stack([corr_real[:energies], corr_imag[:energies]], axis=1)
    greater_lags = jnp.stack([corr_real[energies:], -corr_imag[energies:]], axis=1)
    polar = jnp.stack([lesser_lags, greater_lags], axis=0).astype(jnp.bfloat16)
    returned = lax.all_to_all(polar, "energy", split_axis=1, concat_axis=3, tiled=True)
    returned = returned.reshape(2, energy_local, 2, block_count, block_order, block_order)
    left_product = jnp.einsum(
        "npq,fetnqr->fetnpr", coulomb, returned, preferred_element_type=jnp.float32
    ).astype(jnp.bfloat16)
    screened = jnp.einsum(
        "fetnpr,nsr->fnetps", left_product, coulomb, preferred_element_type=jnp.float32
    )
    return screened.astype(jnp.bfloat16)


def solution(mesh):
    in_specs = (
        P("space", "energy", None, None, None),
        P("space", "energy", None, None, None),
        P("space", "energy", None, None, None),
        P(None, "space", "energy", None, None, None),
        P("space", None, None),
    )
    out_specs = P(None, "space", "energy", None, None, None)
    return jax.shard_map(body, mesh=mesh, in_specs=in_specs, out_specs=out_specs, check_vma=False)
```

profile of v0, /device:TPU:1, one launch (start us, length us, event | category | flops | bytes accessed | tf_op | source)
XLA Modules:
  0.0 188.5 jit_solution(9595420862698619322)
XLA Ops:
  0.0 1.4 copy.66
  1.4 4.5 %collective-permute-start = (bf16[2,1,4,2,128,128]{4,5,0,2,3,1:T(8,128)(2,1)S(1)}, bf16[2,1,4,2,128,128]{4,5,0,2,3,1:T(8,128)(2,1)S(1)}, u32[]{:S(2)}, u32[]{:S(2)}) collective-permute-start(bf16[2,1,4,2,128,128]{4,5,0,2,3,1:T(8,128)(2,1)S(1)} %copy.66), channel_id=1, source_target_pairs={{0,8},{8,16},{16,24},{1,9},{9,17},{17,25},{2,10},{10,18},{18,26},{... | collective-permute-start | bytes 1572872 | tf_op jit(solution)/shard_map/ppermute | solution.py:16
  5.9 1.9 %collective-permute-start.1 = (bf16[2,1,4,2,128,128]{4,5,0,2,3,1:T(8,128)(2,1)S(1)}, bf16[2,1,4,2,128,128]{4,5,0,2,3,1:T(8,128)(2,1)S(1)}, u32[]{:S(2)}, u32[]{:S(2)}) collective-permute-start(bf16[2,1,4,2,128,128]{4,5,0,2,3,1:T(8,128)(2,1)S(1)} %copy.66), channel_id=1, source_target_pairs={{8,0},{16,8},{24,16},{9,1},{17,9},{25,17},{10,2},{18,10},{26,18},{... | collective-permute-start | bytes 1572872 | tf_op jit(solution)/shard_map/ppermute | solution.py:17
  7.8 1.7 slice_bitcast_fusion.13
  9.5 0.9 fusion.133
  10.4 1.6 slice_bitcast_fusion.11
  12.4 2.8 %fusion.4 = f32[4,256,2,128]{3,1,2,0:T(8,128)} fusion(bf16[2,1,4,128,128]{3,4,0,2,1:T(8,128)(2,1)S(1)} %get-tuple-element.19, bf16[2,1,4,128,128]{3,4,0,2,1:T(8,128)(2,1)S(1)} %fusion.136, bf16[2,1,4,128,128]{3,4,0,2,1:T(8,128)(2,1)S(1)} %get-tuple-element.18, bf16[1,4,128,128]{3,2,1,0:T(8,128)(2,1)} %get-tuple-element.29, ...), kind=kOutput, calls=%fused_computation.16 | convolution fusion | flops 275513344 | bytes 2228224 | tf_op jit(solution)/shard_map/fnepr,nesr->fneps/dot_general | solution.py:41
  15.2 3.1 %convolution_add_fusion.5 = f32[4,256,2,128]{3,1,2,0:T(8,128)} fusion(f32[4,256,2,128]{3,1,2,0:T(8,128)} %fusion.4, bf16[2,1,4,128,128]{3,4,0,2,1:T(8,128)(2,1)S(1)} %get-tuple-element.17, bf16[2,1,4,128,128]{3,4,0,2,1:T(8,128)(2,1)S(1)} %fusion.137, bf16[2,1,4,128,128]{3,4,0,2,1:T(8,128)(2,1)S(1)} %get-tuple-element.16, ...), kind=kOutput, calls=%fused_computation.6 | convolution fusion | flops 275775488 | bytes 3276800 | tf_op jit(solution)/shard_map/fnepr,nesr->fneps/dot_general | solution.py:41
  18.4 1.9 fusion
  20.6 9.4 %copy.100 = bf16[1,4,2,1,128,128]{1,2,5,4,3,0:T(2,128)(2,1)} copy(bf16[1,4,2,1,128,128]{5,4,2,1,3,0:T(8,128)(2,1)S(1)} %get-tuple-element.12) | data formatting | bytes 524288 | tf_op jit(solution)/shard_map/squeeze | solution.py:93
  29.9 16.8 %reshape.169 = bf16[8,2,8192]{2,1,0:T(2,128)(2,1)} reshape(bf16[16384,2,4]{2,1,0:T(2,128)(2,1)} %bitcast.216) | data formatting | bytes 524288
  46.7 5.6 %all-to-all-start.1 = ((bf16[8,2,8192]{2,1,0:T(2,128)(2,1)}), bf16[8,2,8192]{2,1,0:T(2,128)(2,1)S(1)}, u32[]{:S(2)}, u32[]{:S(2)}) async-start(bf16[8,2,8192]{2,1,0:T(2,128)(2,1)} %reshape.169), calls=%async_computation.1 | async-start | bytes 524288 | tf_op jit(solution)/shard_map/all_to_all | solution.py:92
  52.8 9.4 %copy.99 = bf16[1,4,2,1,128,128]{1,2,5,4,3,0:T(2,128)(2,1)} copy(bf16[1,4,2,1,128,128]{5,4,2,1,3,0:T(8,128)(2,1)S(1)} %get-tuple-element.13) | data formatting | bytes 524288 | tf_op jit(solution)/shard_map/squeeze | solution.py:90
  62.1 16.8 %reshape.167 = bf16[8,2,8192]{2,1,0:T(2,128)(2,1)} reshape(bf16[16384,2,4]{2,1,0:T(2,128)(2,1)} %bitcast.217) | data formatting | bytes 524288
  79.0 5.4 %all-to-all-start = ((bf16[8,2,8192]{2,1,0:T(2,128)(2,1)}), bf16[8,2,8192]{2,1,0:T(2,128)(2,1)S(1)}, u32[]{:S(2)}, u32[]{:S(2)}) async-start(bf16[8,2,8192]{2,1,0:T(2,128)(2,1)} %reshape.167), calls=%async_computation | async-start | bytes 524288 | tf_op jit(solution)/shard_map/all_to_all | solution.py:89
  84.4 19.1 %reshape.170 = bf16[16384,2,4]{2,1,0:T(2,128)(2,1)} reshape(bf16[8,2,8192]{2,1,0:T(2,128)(2,1)S(1)} %all-to-all-done.1) | data formatting | bytes 524288
  103.5 19.2 %copy.81 = bf16[4,2,8,2048]{3,1,0,2:T(2,128)(2,1)S(1)} copy(bf16[4,2,8,2048]{0,1,3,2:T(2,128)(2,1)} %bitcast.218) | data formatting | bytes 524288 | tf_op jit(solution)/shard_map/all_to_all | solution.py:92
  122.7 0.4 fusion.141
  123.1 0.3 fusion.82
  123.5 0.3 convolution_add_fusion.1
  124.1 0.3 convolution_add_fusion
  124.5 19.1 %reshape.168 = bf16[16384,2,4]{2,1,0:T(2,128)(2,1)} reshape(bf16[8,2,8192]{2,1,0:T(2,128)(2,1)S(1)} %all-to-all-done) | data formatting | bytes 524288
  143.6 19.2 %copy.79 = bf16[4,2,8,2048]{3,1,0,2:T(2,128)(2,1)S(1)} copy(bf16[4,2,8,2048]{0,1,3,2:T(2,128)(2,1)} %bitcast.219) | data formatting | bytes 524288 | tf_op jit(solution)/shard_map/all_to_all | solution.py:89
  162.8 0.4 fusion.142
  163.2 0.3 fusion.88
  163.5 0.3 convolution_add_fusion.3
  164.2 0.3 convolution_add_fusion.2
  164.5 0.3 multiply_add_fusion
  164.8 0.7 fusion.143
  165.7 0.5 copy.82
  166.3 20.3 %all_to_all.51 = bf16[2,32,2,2048]{3,2,0,1:T(2,128)(2,1)S(1)} all-to-all(bf16[2,32,2,2048]{3,2,0,1:T(2,128)(2,1)S(1)} %copy.82), channel_id=1, replica_groups=mesh['space'=4,'energy'=8] {'energy'}, dimensions={1} | all-to-all | bytes 1048576 | tf_op jit(solution)/shard_map/all_to_all | solution.py:128
  187.1 1.4 fusion.2
  (36 shorter events, 2.4 us)
Async XLA Ops:
  0.0 187.1 %copy-start = (bf16[1,128,128]{2,1,0:T(8,128)(2,1)S(1)}, bf16[1,128,128]{2,1,0:T(8,128)(2,1)}, u32[]{:S(2)}) copy-start(bf16[1,128,128]{2,1,0:T(8,128)(2,1)} %param.9) | copy-start | bytes 98308
  0.0 12.1 %copy-start.1 = (bf16[1,4,2,128,128]{4,3,2,1,0:T(8,128)(2,1)S(1)}, bf16[1,4,2,128,128]{4,3,2,1,0:T(8,128)(2,1)}, u32[]{:S(2)}) copy-start(bf16[1,4,2,128,128]{4,3,2,1,0:T(8,128)(2,1)} %param.6) | copy-start | bytes 786436
  0.0 12.1 %copy-start.2 = (bf16[1,4,2,128,128]{4,3,2,1,0:T(8,128)(2,1)S(1)}, bf16[1,4,2,128,128]{4,3,2,1,0:T(8,128)(2,1)}, u32[]{:S(2)}) copy-start(bf16[1,4,2,128,128]{4,3,2,1,0:T(8,128)(2,1)} %param.7) | copy-start | bytes 786436
  1.4 10.9 %collective-permute-start = (bf16[2,1,4,2,128,128]{4,5,0,2,3,1:T(8,128)(2,1)S(1)}, bf16[2,1,4,2,128,128]{4,5,0,2,3,1:T(8,128)(2,1)S(1)}, u32[]{:S(2)}, u32[]{:S(2)}) collective-permute-start(bf16[2,1,4,2,128,128]{4,5,0,2,3,1:T(8,128)(2,1)S(1)} %copy.66), channel_id=1, source_target_pairs={{0,8},{8,16},{16,24},{1,9},{9,17},{17,25},{2,10},{10,18},{18,26},{... | collective-permute-start | bytes 1572872 | tf_op jit(solution)/shard_map/ppermute | solution.py:16
  5.9 12.4 %collective-permute-start.1 = (bf16[2,1,4,2,128,128]{4,5,0,2,3,1:T(8,128)(2,1)S(1)}, bf16[2,1,4,2,128,128]{4,5,0,2,3,1:T(8,128)(2,1)S(1)}, u32[]{:S(2)}, u32[]{:S(2)}) collective-permute-start(bf16[2,1,4,2,128,128]{4,5,0,2,3,1:T(8,128)(2,1)S(1)} %copy.66), channel_id=1, source_target_pairs={{8,0},{16,8},{24,16},{9,1},{17,9},{25,17},{10,2},{18,10},{26,18},{... | collective-permute-start | bytes 1572872 | tf_op jit(solution)/shard_map/ppermute | solution.py:17
  46.7 32.2 %all-to-all-start.1 = ((bf16[8,2,8192]{2,1,0:T(2,128)(2,1)}), bf16[8,2,8192]{2,1,0:T(2,128)(2,1)S(1)}, u32[]{:S(2)}, u32[]{:S(2)}) async-start(bf16[8,2,8192]{2,1,0:T(2,128)(2,1)} %reshape.169), calls=%async_computation.1 | async-start | bytes 524288 | tf_op jit(solution)/shard_map/all_to_all | solution.py:92
  79.0 45.5 %all-to-all-start = ((bf16[8,2,8192]{2,1,0:T(2,128)(2,1)}), bf16[8,2,8192]{2,1,0:T(2,128)(2,1)S(1)}, u32[]{:S(2)}, u32[]{:S(2)}) async-start(bf16[8,2,8192]{2,1,0:T(2,128)(2,1)} %reshape.167), calls=%async_computation | async-start | bytes 524288 | tf_op jit(solution)/shard_map/all_to_all | solution.py:89
where the time goes:
time: 190 us; the launch traced here: 189 us
  local copies, waits for them, and re-layouts  136 us (72%)
  blocking collectives  20.3 us (11%)
  starting transfers between devices  17.4 us (9%)
  matrix products  12.4 us (7%)
  other arithmetic  1.99 us (1%)
    unnamed x11, local copies, waits for them, and re-layouts  73.3 us
    all_to_all x1, blocking collectives, body(): lax.all_to_all(polar, 'energy', split_axis=1, concat_axis=3, tiled=True)  20.3 us
    all_to_all x1, local copies, waits for them, and re-layouts, body(): lax.all_to_all(green_function[0], 'energy', split_axis=2, concat_axis=0,...  19.2 us
    all_to_all x1, local copies, waits for them, and re-layouts, body(): lax.all_to_all(green_function[1], 'energy', split_axis=2, concat_axis=0,...  19.2 us
    squeeze x1, local copies, waits for them, and re-layouts, body(): green_function[1]  9.36 us
    squeeze x1, local copies, waits for them, and re-layouts, body(): green_function[0]  9.36 us
    dot_general x3, matrix products, congruence(): jnp.einsum('fnepr,nesr->fneps', mixed, adjoint_tall, preferred_element_ty...  7.73 us
    all_to_all x1, starting transfers between devices, body(): lax.all_to_all(green_function[1], 'energy', split_axis=2, concat_axis=0,...  5.56 us
  transfers between devices with their start and end apart: 4, of which 0 were waited for; matrix products, arithmetic and copies ran while one was open for 41% of the time, Pallas kernels for 0%

commit v1 on v0

--- a/solution.py
+++ b/solution.py
@@ -1,8 +1,11 @@
+import functools
 import math
 
 import jax
 import jax.numpy as jnp
 from jax import lax
+from jax.experimental import pallas as pl
+from jax.experimental.pallas import tpu as pltpu
 from jax.sharding import PartitionSpec as P
 
 
@@ -61,7 +64,7 @@
     return (out_real, out_imag)
 
 
-def body(green_lower, green_diag, green_upper, self_energy, coulomb):
+def plain_body(green_lower, green_diag, green_upper, self_energy, coulomb):
     block_count = green_diag.shape[0]
     energy_local = green_diag.shape[1]
     block_order = green_diag.shape[-1]
@@ -136,6 +139,304 @@
     return screened.astype(jnp.bfloat16)
 
 
+ROWS = 16
+MESH = pl.DeviceIdType.MESH
+
+
+def partner(me, step):
+    other, bit = me, 1
+    while bit <= step:
+        if step & bit:
+            other = other + bit * (1 - 2 * lax.rem(lax.div(me, bit), 2))
+        bit *= 2
+    return other
+
+
+def far_first(peers):
+    steps, span = [], peers // 2
+    while span >= 1:
+        steps += list(range(span, 2 * span))
+        span //= 2
+    return steps
+
+
+def rotation(real, imag):
+    return jnp.concatenate(
+        [
+            jnp.concatenate([real, imag], axis=1),
+            jnp.concatenate([-imag, real], axis=1),
+        ],
+        axis=0,
+    )
+
+
+def fused_kernel(
+    peers,
+    sites,
+    lower_ref,
+    diag_ref,
+    upper_ref,
+    sigma_ref,
+    coulomb_ref,
+    out_ref,
+    halo,
+    green_out,
+    green_in,
+    series,
+    polar_out,
+    polar_in,
+    halo_send,
+    halo_recv,
+    green_send,
+    green_recv,
+    polar_send,
+    polar_recv,
+):
+    me = lax.axis_index("energy")
+    site = lax.axis_index("space")
+    has_next = site < sites - 1
+    has_previous = site > 0
+    next_site = lax.rem(site + 1, sites)
+    previous_site = lax.rem(site + sites - 1, sites)
+    local = diag_ref.shape[1]
+    order = diag_ref.shape[-1]
+    energies = peers * local
+    steps = far_first(peers)
+    f32 = jnp.float32
+
+    barrier = pltpu.get_barrier_semaphore()
+    for step in steps:
+        pl.semaphore_signal(
+            barrier, inc=1, device_id={"energy": partner(me, step)}, device_id_type=MESH
+        )
+
+    @pl.when(has_next)
+    def _():
+        pl.semaphore_signal(barrier, inc=1, device_id={"space": next_site}, device_id_type=MESH)
+
+    @pl.when(has_previous)
+    def _():
+        pl.semaphore_signal(barrier, inc=1, device_id={"space": previous_site}, device_id_type=MESH)
+
+    neighbours = jnp.where(has_next, 1, 0) + jnp.where(has_previous, 1, 0)
+    pl.semaphore_wait(barrier, peers - 1 + neighbours)
+
+    def halo_copy(side, energy):
+        return pltpu.make_async_remote_copy(
+            src_ref=sigma_ref.at[:, 0, energy],
+            dst_ref=halo.at[side, energy],
+            send_sem=halo_send.at[side, energy],
+            recv_sem=halo_recv.at[side, energy],
+            device_id={"space": next_site if side == 0 else previous_site},
+            device_id_type=MESH,
+        )
+
+    for energy in range(local):
+
+        @pl.when(has_next)
+        def _():
+            halo_copy(0, energy).start()
+
+        @pl.when(has_previous)
+        def _():
+            halo_copy(1, energy).start()
+
+    @pl.when(jnp.logical_not(has_previous))
+    def _():
+        halo[0] = jnp.zeros(halo.shape[1:], halo.dtype)
+
+    @pl.when(jnp.logical_not(has_next))
+    def _():
+        halo[1] = jnp.zeros(halo.shape[1:], halo.dtype)
+
+    def green_copy(other, slot, energy):
+        return pltpu.make_async_remote_copy(
+            src_ref=green_out.at[other, energy],
+            dst_ref=green_in.at[slot, energy],
+            send_sem=green_send.at[other, energy],
+            recv_sem=green_recv.at[slot, energy],
+            device_id={"energy": other},
+            device_id_type=MESH,
+        )
+
+    def one_energy(energy, carry):
+        def term(green_ref, sigma_of):
+            real, imag = green_ref[0, energy, 0], green_ref[0, energy, 1]
+            wide = jnp.concatenate([real, imag], axis=1)
+            mixed = [
+                jnp.dot(
+                    wide,
+                    rotation(sigma_of(kind, 0), sigma_of(kind, 1)),
+                    preferred_element_type=f32,
+                ).astype(jnp.bfloat16)
+                for kind in range(2)
+            ]
+            return lax.dot_general(
+                jnp.concatenate(mixed, axis=0),
+                rotation(real, imag),
+                (((1,), (1,)), ((), ())),
+                preferred_element_type=f32,
+            )
+
+        total = term(diag_ref, lambda kind, part: sigma_ref[kind, 0, energy, part])
+
+        @pl.when(has_previous)
+        def _():
+            halo_copy(0, energy).wait_recv()
+
+        @pl.when(has_next)
+        def _():
+            halo_copy(1, energy).wait_recv()
+
+        total += term(lower_ref, lambda kind, part: halo[0, energy, kind, part])
+        total += term(upper_ref, lambda kind, part: halo[1, energy, kind, part])
+        rounded = total.astype(jnp.bfloat16)
+        for kind in range(2):
+            for part in range(2):
+                block = rounded[
+                    kind * order : (kind + 1) * order, part * order : (part + 1) * order
+                ]
+                green_out[:, energy, kind, part] = block.reshape(peers, ROWS, order)
+        for step in steps:
+            green_copy(partner(me, step), me, energy).start()
+        return carry
+
+    lax.fori_loop(0, local, one_energy, 0)
+
+    tail = series.shape[2] - energies
+    for kind in range(2):
+        for part in range(2):
+            series[kind, part, energies:] = jnp.zeros((tail, ROWS, order), f32)
+
+    def unpack(source, values):
+        for kind in range(2):
+            for part in range(2):
+                series[kind, part, pl.ds(source * local, local)] = values[:, kind, part].astype(f32)
+
+    unpack(me, green_out[me])
+    for step in reversed(steps):
+        other = partner(me, step)
+        for energy in range(local):
+            green_copy(other, other, energy).wait_recv()
+        unpack(other, green_in[other])
+
+    factor = 1.0 / math.sqrt(energies)
+
+    def correlate(kind, owner):
+        first_lag = owner * local
+
+        def some_energies(index, sums):
+            sum_real, sum_imag = sums
+            start = index * local
+            window = pl.ds(start + first_lag, 2 * local - 1)
+            ahead_real, ahead_imag = series[kind, 0, window], series[kind, 1, window]
+            for i in range(local):
+                real, imag = series[1 - kind, 0, start + i], series[1 - kind, 1, start + i]
+                shifted_real, shifted_imag = ahead_real[i : i + local], ahead_imag[i : i + local]
+                sum_real = sum_real + (shifted_real * real + shifted_imag * imag)
+                sum_imag = sum_imag + (shifted_imag * real - shifted_real * imag)
+            return sum_real, sum_imag
+
+        zero = jnp.zeros((local, ROWS, order), f32)
+        sum_real, sum_imag = lax.fori_loop(0, peers - owner, some_energies, (zero, zero))
+        return (sum_real * factor).astype(jnp.bfloat16), (sum_imag * factor).astype(jnp.bfloat16)
+
+    def polar_copy(other, slot, kind):
+        return pltpu.make_async_remote_copy(
+            src_ref=polar_out.at[other, kind],
+            dst_ref=polar_in.at[slot, kind],
+            send_sem=polar_send.at[other, kind],
+            recv_sem=polar_recv.at[slot, kind],
+            device_id={"energy": other},
+            device_id_type=MESH,
+        )
+
+    for kind in range(2):
+        for step in steps:
+            other = partner(me, step)
+            real, imag = correlate(kind, other)
+            polar_out[other, kind, :, 0] = real
+            polar_out[other, kind, :, 1] = imag
+            polar_copy(other, me, kind).start()
+    for kind in range(2):
+        real, imag = correlate(kind, me)
+        polar_in[me, kind, :, 0] = real
+        polar_in[me, kind, :, 1] = imag
+
+    coulomb = coulomb_ref[0]
+    for kind in range(2):
+        for step in steps:
+            other = partner(me, step)
+            polar_copy(other, other, kind).wait_recv()
+        for lag in range(local):
+            both = jnp.concatenate(
+                [polar_in[:, kind, lag, part].reshape(order, order) for part in range(2)], axis=1
+            )
+            left = jnp.dot(coulomb, both, preferred_element_type=f32).astype(jnp.bfloat16)
+            tall = jnp.concatenate([left[:, :order], left[:, order:]], axis=0)
+            screened = lax.dot_general(
+                tall, coulomb, (((1,), (1,)), ((), ())), preferred_element_type=f32
+            ).astype(jnp.bfloat16)
+            out_ref[kind, 0, lag, 0] = screened[:order]
+            out_ref[kind, 0, lag, 1] = screened[order:]
+
+    for energy in range(local):
+
+        @pl.when(has_next)
+        def _():
+            halo_copy(0, energy).wait_send()
+
+        @pl.when(has_previous)
+        def _():
+            halo_copy(1, energy).wait_send()
+
+        for step in steps:
+            green_copy(partner(me, step), me, energy).wait_send()
+    for kind in range(2):
+        for step in steps:
+            polar_copy(partner(me, step), me, kind).wait_send()
+
+
+def fused_body(green_lower, green_diag, green_upper, self_energy, coulomb):
+    peers, sites = lax.axis_size("energy"), lax.axis_size("space")
+    local, order = green_diag.shape[1], green_diag.shape[-1]
+    bf16 = jnp.bfloat16
+    share = (peers, local, 2, 2, ROWS, order)
+    lags = (peers, 2, local, 2, ROWS, order)
+    dma = pltpu.SemaphoreType.DMA
+    return pl.pallas_call(
+        functools.partial(fused_kernel, peers, sites),
+        out_shape=jax.ShapeDtypeStruct(self_energy.shape, bf16),
+        in_specs=[pl.BlockSpec(memory_space=pltpu.VMEM)] * 5,
+        out_specs=pl.BlockSpec(memory_space=pltpu.VMEM),
+        scratch_shapes=[
+            pltpu.VMEM((2, local, 2, 2, order, order), bf16),
+            pltpu.VMEM(share, bf16),
+            pltpu.VMEM(share, bf16),
+            pltpu.VMEM((2, 2, peers * local + local, ROWS, order), jnp.float32),
+            pltpu.VMEM(lags, bf16),
+            pltpu.VMEM(lags, bf16),
+            dma((2, local)),
+            dma((2, local)),
+            dma((peers, local)),
+            dma((peers, local)),
+            dma((peers, 2)),
+            dma((peers, 2)),
+        ],
+        compiler_params=pltpu.CompilerParams(
+            collective_id=0, has_side_effects=True, vmem_limit_bytes=40 * 2**20
+        ),
+    )(green_lower, green_diag, green_upper, self_energy, coulomb)
+
+
+def body(green_lower, green_diag, green_upper, self_energy, coulomb):
+    peers = lax.axis_size("energy")
+    blocks, order = green_diag.shape[0], green_diag.shape[-1]
+    if blocks == 1 and order == peers * ROWS and peers & (peers - 1) == 0:
+        return fused_body(green_lower, green_diag, green_upper, self_energy, coulomb)
+    return plain_body(green_lower, green_diag, green_upper, self_energy, coulomb)
+
+
 def solution(mesh):
     in_specs = (
         P("space", "energy", None, None, None),

time: 190 us -> 39.5 us (0.21)
  local copies, waits for them, and re-layouts: 136 us -> 5.44 us
  Pallas kernels: 0 us -> 33.4 us
  blocking collectives: 20.3 us -> 0 us
  starting transfers between devices: 17.4 us -> 0 us
  matrix products: 12.4 us -> 0 us
  other arithmetic: 1.99 us -> 0 us
    unnamed x11, local copies, waits for them, and re-layouts: 73.3 us -> 5.44 us
    all_to_all x3 -> x0, local copies, waits for them, and re-layouts: 38.7 us -> none  [the longest x1 19.2 us: body(): lax.all_to_all(green_function[0], 'energy', split_axis=2, concat_axis=0,...]
    pallas_call x0 -> x1, Pallas kernels: none -> 33.4 us  [fused_body(): pl.pallas_call(functools.partial(fused_kernel, peers, sites), out_shape=j...]
    squeeze x8 -> x0, local copies, waits for them, and re-layouts: 22.2 us -> none  [the longest x1 9.36 us: body(): green_function[1]]
    all_to_all x1 -> x0, blocking collectives: 20.3 us -> none  [body(): lax.all_to_all(polar, 'energy', split_axis=1, concat_axis=3, tiled=True)]
    dot_general x13 -> x0, matrix products: 12.4 us -> none  [the longest x3 7.73 us: congruence(): jnp.einsum('fnepr,nesr->fneps', mixed, adjoint_tall, preferred_element_ty...]
    all_to_all x2 -> x0, starting transfers between devices: 11 us -> none  [the longest x1 5.56 us: body(): lax.all_to_all(green_function[1], 'energy', split_axis=2, concat_axis=0,...]
    ppermute x2 -> x0, starting transfers between devices: 6.43 us -> none  [the longest x1 4.51 us: padded_2(): before = lax.ppermute(last, axis, up)]
  transfers between devices with their start and end apart: 4 -> 0, of which waited for: 0 -> 0; matrix products, arithmetic and copies ran while one was open for 41% -> 0% of each run, Pallas kernels for 0% -> 0%
where the time goes in v1:
time: 39.5 us; the launch traced here: 38.9 us
  Pallas kernels  33.4 us (85%)
  local copies, waits for them, and re-layouts  5.44 us (14%)
    pallas_call x1, Pallas kernels, fused_body(): pl.pallas_call(functools.partial(fused_kernel, peers, sites), out_shape=j...  33.4 us
    unnamed x11, local copies, waits for them, and re-layouts  5.44 us

profile of v1, /device:TPU:1, one launch (start us, length us, event | category | flops | bytes accessed | tf_op | source)
XLA Modules:
  0.0 38.9 jit_solution(2427173637931477711)
XLA Ops:
  0.0 0.0 copy-start
  0.0 1.0 %copy-done = bf16[2,1,4,2,128,128]{5,4,3,2,1,0:T(8,128)(2,1)S(1)} copy-done((bf16[2,1,4,2,128,128]{5,4,3,2,1,0:T(8,128)(2,1)S(1)}, bf16[2,1,4,2,128,128]{5,4,3,2,1,0:T(8,128)(2,1)}, u32[]{:S(2)}) %copy-start) | copy-done | bytes 524312
  1.0 0.0 copy-start.1
  1.0 0.9 %copy-done.1 = bf16[1,4,2,128,128]{4,3,2,1,0:T(8,128)(2,1)S(1)} copy-done((bf16[1,4,2,128,128]{4,3,2,1,0:T(8,128)(2,1)S(1)}, bf16[1,4,2,128,128]{4,3,2,1,0:T(8,128)(2,1)}, u32[]{:S(2)}) %copy-start.1) | copy-done | bytes 262168
  2.0 0.0 copy-start.2
  2.0 0.9 %copy-done.2 = bf16[1,4,2,128,128]{4,3,2,1,0:T(8,128)(2,1)S(1)} copy-done((bf16[1,4,2,128,128]{4,3,2,1,0:T(8,128)(2,1)S(1)}, bf16[1,4,2,128,128]{4,3,2,1,0:T(8,128)(2,1)}, u32[]{:S(2)}) %copy-start.2) | copy-done | bytes 262168
  2.9 0.0 copy-start.3
  2.9 0.9 %copy-done.3 = bf16[1,4,2,128,128]{4,3,2,1,0:T(8,128)(2,1)S(1)} copy-done((bf16[1,4,2,128,128]{4,3,2,1,0:T(8,128)(2,1)S(1)}, bf16[1,4,2,128,128]{4,3,2,1,0:T(8,128)(2,1)}, u32[]{:S(2)}) %copy-start.3) | copy-done | bytes 262168
  3.9 0.0 copy-start.4
  3.9 0.8 %copy-done.4 = bf16[1,128,128]{2,1,0:T(8,128)(2,1)S(1)} copy-done((bf16[1,128,128]{2,1,0:T(8,128)(2,1)S(1)}, bf16[1,128,128]{2,1,0:T(8,128)(2,1)}, u32[]{:S(2)}) %copy-start.4) | copy-done | bytes 32792
  4.7 33.4 %shard_map.55 = bf16[2,1,4,2,128,128]{5,4,3,2,1,0:T(8,128)(2,1)S(1)} custom-call(bf16[1,4,2,128,128]{4,3,2,1,0:T(8,128)(2,1)S(1)} %copy-done.1, bf16[1,4,2,128,128]{4,3,2,1,0:T(8,128)(2,1)S(1)} %copy-done.2, bf16[1,4,2,128,128]{4,3,2,1,0:T(8,128)(2,1)S(1)} %copy-done.3, bf16[2,1,4,2,128,128]{5,4,3,2,1,0:T(8,128)(2,1)S(1)} %copy-done, ...), custom_call_target="tpu_custom_call" | custom-call | tf_op jit(solution)/shard_map/pallas_call | solution.py:407
  38.1 0.8 %copy.7 = bf16[2,1,4,2,128,128]{5,4,3,2,1,0:T(8,128)(2,1)} copy(bf16[2,1,4,2,128,128]{5,4,3,2,1,0:T(8,128)(2,1)S(1)} %shard_map.55) | data formatting | bytes 1048576
Async XLA Ops:
  0.0 1.0 %copy-start = (bf16[2,1,4,2,128,128]{5,4,3,2,1,0:T(8,128)(2,1)S(1)}, bf16[2,1,4,2,128,128]{5,4,3,2,1,0:T(8,128)(2,1)}, u32[]{:S(2)}) copy-start(bf16[2,1,4,2,128,128]{5,4,3,2,1,0:T(8,128)(2,1)} %sigma_ref.1) | copy-start | bytes 1572868
  1.0 0.9 %copy-start.1 = (bf16[1,4,2,128,128]{4,3,2,1,0:T(8,128)(2,1)S(1)}, bf16[1,4,2,128,128]{4,3,2,1,0:T(8,128)(2,1)}, u32[]{:S(2)}) copy-start(bf16[1,4,2,128,128]{4,3,2,1,0:T(8,128)(2,1)} %lower_ref.1) | copy-start | bytes 786436
  2.0 0.9 %copy-start.2 = (bf16[1,4,2,128,128]{4,3,2,1,0:T(8,128)(2,1)S(1)}, bf16[1,4,2,128,128]{4,3,2,1,0:T(8,128)(2,1)}, u32[]{:S(2)}) copy-start(bf16[1,4,2,128,128]{4,3,2,1,0:T(8,128)(2,1)} %diag_ref.1) | copy-start | bytes 786436
  2.9 0.9 %copy-start.3 = (bf16[1,4,2,128,128]{4,3,2,1,0:T(8,128)(2,1)S(1)}, bf16[1,4,2,128,128]{4,3,2,1,0:T(8,128)(2,1)}, u32[]{:S(2)}) copy-start(bf16[1,4,2,128,128]{4,3,2,1,0:T(8,128)(2,1)} %upper_ref.1) | copy-start | bytes 786436
  3.9 0.8 %copy-start.4 = (bf16[1,128,128]{2,1,0:T(8,128)(2,1)S(1)}, bf16[1,128,128]{2,1,0:T(8,128)(2,1)}, u32[]{:S(2)}) copy-start(bf16[1,128,128]{2,1,0:T(8,128)(2,1)} %coulomb_ref.1) | copy-start | bytes 98308

commit v2 on v1

--- a/solution.py
+++ b/solution.py
@@ -173,18 +173,25 @@
 def fused_kernel(
     peers,
     sites,
+    lower_hbm,
+    diag_hbm,
+    upper_hbm,
+    sigma_hbm,
+    coulomb_hbm,
+    out_ref,
     lower_ref,
     diag_ref,
     upper_ref,
     sigma_ref,
     coulomb_ref,
-    out_ref,
     halo,
     green_out,
     green_in,
     series,
     polar_out,
     polar_in,
+    load_sem,
+    coulomb_sem,
     halo_send,
     halo_recv,
     green_send,
@@ -198,11 +205,11 @@
     has_previous = site > 0
     next_site = lax.rem(site + 1, sites)
     previous_site = lax.rem(site + sites - 1, sites)
-    local = diag_ref.shape[1]
-    order = diag_ref.shape[-1]
+    local, order = diag_ref.shape[0], diag_ref.shape[-1]
+    half = order // 2
     energies = peers * local
     steps = far_first(peers)
-    f32 = jnp.float32
+    f32, bf16 = jnp.float32, jnp.bfloat16
 
     barrier = pltpu.get_barrier_semaphore()
     for step in steps:
@@ -218,12 +225,30 @@
     def _():
         pl.semaphore_signal(barrier, inc=1, device_id={"space": previous_site}, device_id_type=MESH)
 
+    def loads(energy):
+        pairs = [
+            (diag_hbm.at[0, energy], diag_ref.at[energy]),
+            (sigma_hbm.at[:, 0, energy], sigma_ref.at[:, energy]),
+            (lower_hbm.at[0, energy], lower_ref.at[energy]),
+            (upper_hbm.at[0, energy], upper_ref.at[energy]),
+        ]
+        return [
+            pltpu.make_async_copy(source, target, load_sem.at[energy, i])
+            for i, (source, target) in enumerate(pairs)
+        ]
+
+    for energy in range(local):
+        for load in loads(energy):
+            load.start()
+    coulomb_load = pltpu.make_async_copy(coulomb_hbm.at[0], coulomb_ref, coulomb_sem)
+    coulomb_load.start()
+
     neighbours = jnp.where(has_next, 1, 0) + jnp.where(has_previous, 1, 0)
     pl.semaphore_wait(barrier, peers - 1 + neighbours)
 
     def halo_copy(side, energy):
         return pltpu.make_async_remote_copy(
-            src_ref=sigma_ref.at[:, 0, energy],
+            src_ref=sigma_hbm.at[:, 0, energy],
             dst_ref=halo.at[side, energy],
             send_sem=halo_send.at[side, energy],
             recv_sem=halo_recv.at[side, energy],
@@ -249,36 +274,50 @@
     def _():
         halo[1] = jnp.zeros(halo.shape[1:], halo.dtype)
 
-    def green_copy(other, slot, energy):
+    def green_copy(side, other, slot, first, count):
         return pltpu.make_async_remote_copy(
-            src_ref=green_out.at[other, energy],
-            dst_ref=green_in.at[slot, energy],
-            send_sem=green_send.at[other, energy],
-            recv_sem=green_recv.at[slot, energy],
+            src_ref=green_out.at[side, other, pl.ds(first, count)],
+            dst_ref=green_in.at[side, slot, pl.ds(first, count)],
+            send_sem=green_send.at[side, other, first],
+            recv_sem=green_recv.at[side, slot, first],
             device_id={"energy": other},
             device_id_type=MESH,
         )
 
-    def one_energy(energy, carry):
-        def term(green_ref, sigma_of):
-            real, imag = green_ref[0, energy, 0], green_ref[0, energy, 1]
-            wide = jnp.concatenate([real, imag], axis=1)
-            mixed = [
-                jnp.dot(
-                    wide,
-                    rotation(sigma_of(kind, 0), sigma_of(kind, 1)),
-                    preferred_element_type=f32,
-                ).astype(jnp.bfloat16)
-                for kind in range(2)
-            ]
-            return lax.dot_general(
-                jnp.concatenate(mixed, axis=0),
-                rotation(real, imag),
-                (((1,), (1,)), ((), ())),
+    parts = [
+        [(energy, 1) for energy in range(local)],
+        [(0, 1)] + ([(1, local - 1)] if local > 1 else []),
+    ]
+
+    def send_green(side, first, count):
+        for step in steps:
+            green_copy(side, partner(me, step), me, first, count).start()
+
+    def term(green_ref, energy, sigma_of):
+        real, imag = green_ref[energy, 0], green_ref[energy, 1]
+        wide = jnp.concatenate([real, imag], axis=1)
+        mixed = [
+            jnp.dot(
+                wide,
+                rotation(sigma_of(kind, 0), sigma_of(kind, 1)),
                 preferred_element_type=f32,
-            )
-
-        total = term(diag_ref, lambda kind, part: sigma_ref[kind, 0, energy, part])
+            ).astype(bf16)
+            for kind in range(2)
+        ]
+        adjoint = jnp.concatenate(
+            [rotation(real[:half], imag[:half]), rotation(real[half:], imag[half:])], axis=0
+        )
+        return lax.dot_general(
+            jnp.concatenate(mixed, axis=0),
+            adjoint,
+            (((1,), (1,)), ((), ())),
+            preferred_element_type=f32,
+        )
+
+    for energy in range(local):
+        for load in loads(energy):
+            load.wait()
+        total = term(diag_ref, energy, lambda kind, part: sigma_ref[kind, energy, part])
 
         @pl.when(has_previous)
         def _():
@@ -288,97 +327,145 @@
         def _():
             halo_copy(1, energy).wait_recv()
 
-        total += term(lower_ref, lambda kind, part: halo[0, energy, kind, part])
-        total += term(upper_ref, lambda kind, part: halo[1, energy, kind, part])
-        rounded = total.astype(jnp.bfloat16)
+        total += term(lower_ref, energy, lambda kind, part: halo[0, energy, kind, part])
+        total += term(upper_ref, energy, lambda kind, part: halo[1, energy, kind, part])
+        rounded = total.astype(bf16)
+        for side in range(2):
+            for kind in range(2):
+                block = rounded[
+                    kind * order : (kind + 1) * order, side * order : (side + 1) * order
+                ]
+                green_out[side, :, energy, kind] = block.reshape(peers, ROWS, order)
+        send_green(0, energy, 1)
+        if energy == 0:
+            send_green(1, 0, 1)
+    if local > 1:
+        send_green(1, *parts[1][1])
+
+    coulomb_load.wait()
+    coulomb = coulomb_ref[...]
+    in_low = lax.broadcasted_iota(jnp.int32, (order, order), 1) < half
+    straight = coulomb.astype(f32)
+    swapped = pltpu.roll(straight, half, 1)
+    zeros = jnp.zeros_like(straight)
+    spread = jnp.concatenate(
+        [
+            jnp.concatenate(
+                [jnp.where(in_low, straight, zeros), jnp.where(in_low, swapped, zeros)], axis=1
+            ),
+            jnp.concatenate(
+                [jnp.where(in_low, zeros, swapped), jnp.where(in_low, zeros, straight)], axis=1
+            ),
+        ],
+        axis=0,
+    ).astype(bf16)
+
+    fold = ROWS // 2
+    low_lanes = lax.broadcasted_iota(jnp.int32, (local, fold, order), 2) < half
+
+    def swap(values):
+        return pltpu.roll(values.reshape(-1, order), half, 1).reshape(values.shape)
+
+    tail = series.shape[3] - energies
+    for side in range(2):
         for kind in range(2):
             for part in range(2):
-                block = rounded[
-                    kind * order : (kind + 1) * order, part * order : (part + 1) * order
-                ]
-                green_out[:, energy, kind, part] = block.reshape(peers, ROWS, order)
+                series[side, kind, part, energies:] = jnp.zeros((tail, fold, order), f32)
+
+    def unpack(side, source, values):
+        for kind in range(2):
+            tile = values[:, kind].astype(f32)
+            top, bottom = tile[:, :fold], tile[:, fold:]
+            where = pl.ds(source * local, local)
+            series[side, kind, 0, where] = jnp.where(low_lanes, top, swap(bottom))
+            series[side, kind, 1, where] = jnp.where(low_lanes, swap(top), bottom)
+
+    def receive_green(side):
+        unpack(side, me, green_out[side, me])
         for step in steps:
-            green_copy(partner(me, step), me, energy).start()
-        return carry
-
-    lax.fori_loop(0, local, one_energy, 0)
-
-    tail = series.shape[2] - energies
-    for kind in range(2):
-        for part in range(2):
-            series[kind, part, energies:] = jnp.zeros((tail, ROWS, order), f32)
-
-    def unpack(source, values):
-        for kind in range(2):
-            for part in range(2):
-                series[kind, part, pl.ds(source * local, local)] = values[:, kind, part].astype(f32)
-
-    unpack(me, green_out[me])
-    for step in reversed(steps):
-        other = partner(me, step)
-        for energy in range(local):
-            green_copy(other, other, energy).wait_recv()
-        unpack(other, green_in[other])
+            other = partner(me, step)
+            for first, count in parts[side]:
+                green_copy(side, other, other, first, count).wait_recv()
+            unpack(side, other, green_in[side, other])
 
     factor = 1.0 / math.sqrt(energies)
 
-    def correlate(kind, owner):
+    def correlate(side, owner):
         first_lag = owner * local
 
         def some_energies(index, sums):
-            sum_real, sum_imag = sums
             start = index * local
             window = pl.ds(start + first_lag, 2 * local - 1)
-            ahead_real, ahead_imag = series[kind, 0, window], series[kind, 1, window]
-            for i in range(local):
-                real, imag = series[1 - kind, 0, start + i], series[1 - kind, 1, start + i]
-                shifted_real, shifted_imag = ahead_real[i : i + local], ahead_imag[i : i + local]
-                sum_real = sum_real + (shifted_real * real + shifted_imag * imag)
-                sum_imag = sum_imag + (shifted_imag * real - shifted_real * imag)
-            return sum_real, sum_imag
-
-        zero = jnp.zeros((local, ROWS, order), f32)
-        sum_real, sum_imag = lax.fori_loop(0, peers - owner, some_energies, (zero, zero))
-        return (sum_real * factor).astype(jnp.bfloat16), (sum_imag * factor).astype(jnp.bfloat16)
-
-    def polar_copy(other, slot, kind):
+            results = []
+            for kind in range(2):
+                sum_real, sum_imag = sums[2 * kind : 2 * kind + 2]
+                ahead_real, ahead_imag = series[side, kind, 0, window], series[side, kind, 1, window]
+                for i in range(local):
+                    real = series[side, 1 - kind, 0, start + i]
+                    imag = series[side, 1 - kind, 1, start + i]
+                    shifted_real, shifted_imag = ahead_real[i : i + local], ahead_imag[i : i + local]
+                    sum_real = sum_real + (shifted_real * real + shifted_imag * imag)
+                    sum_imag = sum_imag + (shifted_imag * real - shifted_real * imag)
+                results += [sum_real, sum_imag]
+            return tuple(results)
+
+        zero = jnp.zeros((local, fold, order), f32)
+        sums = lax.fori_loop(0, peers - owner, some_energies, (zero,) * 4)
+        tiles = []
+        for kind in range(2):
+            real, imag = sums[2 * kind] * factor, sums[2 * kind + 1] * factor
+            top = jnp.where(low_lanes, real, swap(imag))
+            bottom = jnp.where(low_lanes, swap(real), imag)
+            tiles.append(jnp.concatenate([top, bottom], axis=1).astype(bf16))
+        return tiles
+
+    def polar_copy(side, other, slot, kind):
         return pltpu.make_async_remote_copy(
-            src_ref=polar_out.at[other, kind],
-            dst_ref=polar_in.at[slot, kind],
-            send_sem=polar_send.at[other, kind],
-            recv_sem=polar_recv.at[slot, kind],
+            src_ref=polar_out.at[side, other, kind],
+            dst_ref=polar_in.at[side, slot, kind],
+            send_sem=polar_send.at[side, other, kind],
+            recv_sem=polar_recv.at[side, slot, kind],
             device_id={"energy": other},
             device_id_type=MESH,
         )
 
-    for kind in range(2):
+    for side in range(2):
+        receive_green(side)
         for step in steps:
             other = partner(me, step)
-            real, imag = correlate(kind, other)
-            polar_out[other, kind, :, 0] = real
-            polar_out[other, kind, :, 1] = imag
-            polar_copy(other, me, kind).start()
+            tiles = correlate(side, other)
+            for kind in range(2):
+                polar_out[side, other, kind] = tiles[kind]
+            for kind in range(2 if side == 0 else 1):
+                polar_copy(side, other, me, kind).start()
+        if side == 1:
+            for step in steps:
+                polar_copy(side, partner(me, step), me, 1).start()
+        tiles = correlate(side, me)
+        for kind in range(2):
+            polar_in[side, me, kind] = tiles[kind]
+
     for kind in range(2):
-        real, imag = correlate(kind, me)
-        polar_in[me, kind, :, 0] = real
-        polar_in[me, kind, :, 1] = imag
-
-    coulomb = coulomb_ref[0]
-    for kind in range(2):
-        for step in steps:
-            other = partner(me, step)
-            polar_copy(other, other, kind).wait_recv()
+        for side in range(2):
+            for step in steps:
+                other = partner(me, step)
+                polar_copy(side, other, other, kind).wait_recv()
+        lefts = []
         for lag in range(local):
             both = jnp.concatenate(
-                [polar_in[:, kind, lag, part].reshape(order, order) for part in range(2)], axis=1
+                [polar_in[side, :, kind, lag].reshape(order, order) for side in range(2)], axis=1
             )
-            left = jnp.dot(coulomb, both, preferred_element_type=f32).astype(jnp.bfloat16)
-            tall = jnp.concatenate([left[:, :order], left[:, order:]], axis=0)
-            screened = lax.dot_general(
-                tall, coulomb, (((1,), (1,)), ((), ())), preferred_element_type=f32
-            ).astype(jnp.bfloat16)
-            out_ref[kind, 0, lag, 0] = screened[:order]
-            out_ref[kind, 0, lag, 1] = screened[order:]
+            lefts.append(jnp.dot(coulomb, both, preferred_element_type=f32).astype(bf16))
+        screened = lax.dot_general(
+            jnp.concatenate(lefts, axis=0),
+            spread,
+            (((1,), (1,)), ((), ())),
+            preferred_element_type=f32,
+        ).astype(bf16)
+        for lag in range(local):
+            rows = screened[lag * order : (lag + 1) * order]
+            out_ref[kind, 0, lag, 0] = rows[:, :order]
+            out_ref[kind, 0, lag, 1] = rows[:, order:]
 
     for energy in range(local):
 
@@ -390,38 +477,46 @@
         def _():
             halo_copy(1, energy).wait_send()
 
+    for side in range(2):
         for step in steps:
-            green_copy(partner(me, step), me, energy).wait_send()
-    for kind in range(2):
-        for step in steps:
-            polar_copy(partner(me, step), me, kind).wait_send()
+            other = partner(me, step)
+            for first, count in parts[side]:
+                green_copy(side, other, me, first, count).wait_send()
+            for kind in range(2):
+                polar_copy(side, other, me, kind).wait_send()
 
 
 def fused_body(green_lower, green_diag, green_upper, self_energy, coulomb):
     peers, sites = lax.axis_size("energy"), lax.axis_size("space")
     local, order = green_diag.shape[1], green_diag.shape[-1]
     bf16 = jnp.bfloat16
-    share = (peers, local, 2, 2, ROWS, order)
-    lags = (peers, 2, local, 2, ROWS, order)
+    share = (2, peers, local, 2, ROWS, order)
+    lags = (2, peers, 2, local, ROWS, order)
+    series = (2, 2, 2, peers * local + local, ROWS // 2, order)
     dma = pltpu.SemaphoreType.DMA
     return pl.pallas_call(
         functools.partial(fused_kernel, peers, sites),
         out_shape=jax.ShapeDtypeStruct(self_energy.shape, bf16),
-        in_specs=[pl.BlockSpec(memory_space=pltpu.VMEM)] * 5,
+        in_specs=[pl.BlockSpec(memory_space=pltpu.HBM)] * 5,
         out_specs=pl.BlockSpec(memory_space=pltpu.VMEM),
-        scratch_shapes=[
+        scratch_shapes=[pltpu.VMEM((local, 2, order, order), bf16)] * 3
+        + [
+            pltpu.VMEM((2, local, 2, order, order), bf16),
+            pltpu.VMEM((order, order), bf16),
             pltpu.VMEM((2, local, 2, 2, order, order), bf16),
             pltpu.VMEM(share, bf16),
             pltpu.VMEM(share, bf16),
-            pltpu.VMEM((2, 2, peers * local + local, ROWS, order), jnp.float32),
+            pltpu.VMEM(series, jnp.float32),
             pltpu.VMEM(lags, bf16),
             pltpu.VMEM(lags, bf16),
+            dma((local, 4)),
+            dma,
             dma((2, local)),
             dma((2, local)),
-            dma((peers, local)),
-            dma((peers, local)),
-            dma((peers, 2)),
-            dma((peers, 2)),
+            dma((2, peers, local)),
+            dma((2, peers, local)),
+            dma((2, peers, 2)),
+            dma((2, peers, 2)),
         ],
         compiler_params=pltpu.CompilerParams(
             collective_id=0, has_side_effects=True, vmem_limit_bytes=40 * 2**20
@@ -432,7 +527,7 @@
 def body(green_lower, green_diag, green_upper, self_energy, coulomb):
     peers = lax.axis_size("energy")
     blocks, order = green_diag.shape[0], green_diag.shape[-1]
-    if blocks == 1 and order == peers * ROWS and peers & (peers - 1) == 0:
+    if blocks == 1 and order == 128 and order == peers * ROWS and peers & (peers - 1) == 0:
         return fused_body(green_lower, green_diag, green_upper, self_energy, coulomb)
     return plain_body(green_lower, green_diag, green_upper, self_energy, coulomb)
 

time: 39.5 us -> 40.2 us (1.018)
  Pallas kernels: 33.4 us -> 34.4 us
    pallas_call x1, Pallas kernels: 33.4 us -> 34.4 us  [fused_body(): pl.pallas_call(functools.partial(fused_kernel, peers, sites), out_shape=j...]
where the time goes in v2:
time: 40.2 us; the launch traced here: 39.8 us
  Pallas kernels  34.4 us (86%)
  local copies, waits for them, and re-layouts  5.44 us (14%)
    pallas_call x1, Pallas kernels, fused_body(): pl.pallas_call(functools.partial(fused_kernel, peers, sites), out_shape=j...  34.4 us
    unnamed x11, local copies, waits for them, and re-layouts  5.44 us

profile of v2, /device:TPU:1, one launch (start us, length us, event | category | flops | bytes accessed | tf_op | source)
XLA Modules:
  0.0 39.8 jit_solution(9324863397414504298)
XLA Ops:
  0.0 0.0 copy-start
  0.0 1.0 %copy-done = bf16[2,1,4,2,128,128]{5,4,3,2,1,0:T(8,128)(2,1)S(1)} copy-done((bf16[2,1,4,2,128,128]{5,4,3,2,1,0:T(8,128)(2,1)S(1)}, bf16[2,1,4,2,128,128]{5,4,3,2,1,0:T(8,128)(2,1)}, u32[]{:S(2)}) %copy-start) | copy-done | bytes 524312
  1.0 0.0 copy-start.1
  1.0 0.9 %copy-done.1 = bf16[1,4,2,128,128]{4,3,2,1,0:T(8,128)(2,1)S(1)} copy-done((bf16[1,4,2,128,128]{4,3,2,1,0:T(8,128)(2,1)S(1)}, bf16[1,4,2,128,128]{4,3,2,1,0:T(8,128)(2,1)}, u32[]{:S(2)}) %copy-start.1) | copy-done | bytes 262168
  2.0 0.0 copy-start.2
  2.0 0.9 %copy-done.2 = bf16[1,4,2,128,128]{4,3,2,1,0:T(8,128)(2,1)S(1)} copy-done((bf16[1,4,2,128,128]{4,3,2,1,0:T(8,128)(2,1)S(1)}, bf16[1,4,2,128,128]{4,3,2,1,0:T(8,128)(2,1)}, u32[]{:S(2)}) %copy-start.2) | copy-done | bytes 262168
  2.9 0.0 copy-start.3
  2.9 0.9 %copy-done.3 = bf16[1,4,2,128,128]{4,3,2,1,0:T(8,128)(2,1)S(1)} copy-done((bf16[1,4,2,128,128]{4,3,2,1,0:T(8,128)(2,1)S(1)}, bf16[1,4,2,128,128]{4,3,2,1,0:T(8,128)(2,1)}, u32[]{:S(2)}) %copy-start.3) | copy-done | bytes 262168
  3.9 0.0 copy-start.4
  3.9 0.8 %copy-done.4 = bf16[1,128,128]{2,1,0:T(8,128)(2,1)S(1)} copy-done((bf16[1,128,128]{2,1,0:T(8,128)(2,1)S(1)}, bf16[1,128,128]{2,1,0:T(8,128)(2,1)}, u32[]{:S(2)}) %copy-start.4) | copy-done | bytes 32792
  4.7 34.4 %shard_map.55 = bf16[2,1,4,2,128,128]{5,4,3,2,1,0:T(8,128)(2,1)S(1)} custom-call(bf16[1,4,2,128,128]{4,3,2,1,0:T(8,128)(2,1)S(1)} %copy-done.1, bf16[1,4,2,128,128]{4,3,2,1,0:T(8,128)(2,1)S(1)} %copy-done.2, bf16[1,4,2,128,128]{4,3,2,1,0:T(8,128)(2,1)S(1)} %copy-done.3, bf16[2,1,4,2,128,128]{5,4,3,2,1,0:T(8,128)(2,1)S(1)} %copy-done, ...), custom_call_target="tpu_custom_call" | custom-call | tf_op jit(solution)/shard_map/pallas_call | solution.py:497
  39.0 0.8 %copy.7 = bf16[2,1,4,2,128,128]{5,4,3,2,1,0:T(8,128)(2,1)} copy(bf16[2,1,4,2,128,128]{5,4,3,2,1,0:T(8,128)(2,1)S(1)} %shard_map.55) | data formatting | bytes 1048576
Async XLA Ops:
  0.0 1.0 %copy-start = (bf16[2,1,4,2,128,128]{5,4,3,2,1,0:T(8,128)(2,1)S(1)}, bf16[2,1,4,2,128,128]{5,4,3,2,1,0:T(8,128)(2,1)}, u32[]{:S(2)}) copy-start(bf16[2,1,4,2,128,128]{5,4,3,2,1,0:T(8,128)(2,1)} %sigma_hbm.1) | copy-start | bytes 1572868
  1.0 0.9 %copy-start.1 = (bf16[1,4,2,128,128]{4,3,2,1,0:T(8,128)(2,1)S(1)}, bf16[1,4,2,128,128]{4,3,2,1,0:T(8,128)(2,1)}, u32[]{:S(2)}) copy-start(bf16[1,4,2,128,128]{4,3,2,1,0:T(8,128)(2,1)} %lower_hbm.1) | copy-start | bytes 786436
  2.0 0.9 %copy-start.2 = (bf16[1,4,2,128,128]{4,3,2,1,0:T(8,128)(2,1)S(1)}, bf16[1,4,2,128,128]{4,3,2,1,0:T(8,128)(2,1)}, u32[]{:S(2)}) copy-start(bf16[1,4,2,128,128]{4,3,2,1,0:T(8,128)(2,1)} %diag_hbm.1) | copy-start | bytes 786436
  2.9 0.9 %copy-start.3 = (bf16[1,4,2,128,128]{4,3,2,1,0:T(8,128)(2,1)S(1)}, bf16[1,4,2,128,128]{4,3,2,1,0:T(8,128)(2,1)}, u32[]{:S(2)}) copy-start(bf16[1,4,2,128,128]{4,3,2,1,0:T(8,128)(2,1)} %upper_hbm.1) | copy-start | bytes 786436
  3.9 0.8 %copy-start.4 = (bf16[1,128,128]{2,1,0:T(8,128)(2,1)S(1)}, bf16[1,128,128]{2,1,0:T(8,128)(2,1)}, u32[]{:S(2)}) copy-start(bf16[1,128,128]{2,1,0:T(8,128)(2,1)} %coulomb_hbm.1) | copy-start | bytes 98308
